TPU v7x, 512 devices: a whole 4x8x8 slice. The times are simulated.
512 devices in a mesh: row: 8 (over x, core), col: 16 (over y_lo, z), layer: 4 (over y_hi).
Axes of the slice: x: 4, y: 8 (y_hi: 4, y_lo: 2; y = y_hi * 2 + y_lo), z: 8, core: 2. Of those that a mesh axis runs over, the one named last changes fastest.
Arguments:
- hamiltonian: bfloat16 [8192, 8192], P('row', ('col', 'layer')), as said below
- inv_root: bfloat16 [8192, 8192], P('row', 'col'), as said below
- h_pattern: int32 [32, 32], replicated, may hold values from 0 to 1, as said below
- z_pattern: int32 [32, 32], replicated, may hold values from 0 to 1, as said below
Outputs:
- transformed: bfloat16 [8192, 8192], P('row', ('col', 'layer'))
Inputs may be any that keep to these rules, and one draw needn't show every extreme that they name: hamiltonian is symmetric. inv_root is symmetric. h_pattern is symmetric and every diagonal block is present. z_pattern is symmetric and every diagonal block is present.
All inputs are finite; a program needn't handle non-finite values.
Results may differ from a plain program's by a relative error of at most 0.005.
Values may be sent and summed in bfloat16 or wider, within the bound.
A program may use at most 64 MiB of HBM per device.

v0:
```python
import jax
import jax.numpy as jnp
from jax import lax
from jax.sharding import PartitionSpec as P

BS = 256


def mask_tile(tile, pattern, row_start, col_start):
    blocks = pattern.shape[0]
    block_ids = jnp.arange(blocks, dtype=jnp.int32)
    row_ids = (row_start + jnp.arange(tile.shape[0], dtype=jnp.int32)) // BS
    col_ids = (col_start + jnp.arange(tile.shape[1], dtype=jnp.int32)) // BS
    row_pick = (row_ids[:, None] == block_ids[None, :]).astype(jnp.float32)
    col_pick = (block_ids[:, None] == col_ids[None, :]).astype(jnp.float32)
    inner = jnp.dot(pattern.astype(jnp.float32), col_pick, precision=lax.Precision.HIGHEST)
    keep = jnp.dot(row_pick, inner, precision=lax.Precision.HIGHEST)
    return jnp.where(keep > 0.5, tile, jnp.zeros_like(tile))


def accumulate(left, right):
    return jnp.dot(left, right, preferred_element_type=jnp.float32)


def local(hamiltonian, inv_root, h_pattern, z_pattern):
    rows_here = inv_root.shape[0]
    cols_here = inv_root.shape[1]
    quarter = hamiltonian.shape[1]
    layers = lax.axis_size("layer")
    per_row = lax.axis_size("col") // lax.axis_size("row")
    row_index = lax.axis_index("row")
    col_index = lax.axis_index("col")
    layer_index = lax.axis_index("layer")
    h_local = mask_tile(
        hamiltonian, h_pattern, row_index * rows_here, col_index * cols_here + layer_index * quarter
    )
    z_local = mask_tile(inv_root, z_pattern, row_index * rows_here, col_index * cols_here)
    h_whole = lax.all_gather(h_local, "col", axis=1, tiled=True)
    z_layered = z_local.reshape(per_row, layers, quarter, cols_here)
    z_part = lax.dynamic_index_in_dim(z_layered, layer_index, 1, keepdims=False).reshape(
        per_row * quarter, cols_here
    )
    columns = h_whole
    partial_y = accumulate(columns, lax.all_gather(z_part, "row", axis=0, tiled=True))
    z_quarter = lax.dynamic_slice_in_dim(z_local, layer_index * quarter, quarter, 1)
    z_rows = lax.all_gather(z_quarter, "col", axis=1, tiled=True)
    summed = lax.psum(partial_y, "layer")
    layered = summed.reshape(per_row, layers, quarter, cols_here)
    own_rows = lax.dynamic_index_in_dim(layered, layer_index, 1, keepdims=False).reshape(
        per_row * quarter, cols_here
    )
    y_own = own_rows.astype(jnp.bfloat16)
    columns = z_rows
    partial_c = accumulate(columns, lax.all_gather(y_own, "row", axis=0, tiled=True))
    result = lax.psum_scatter(partial_c, "layer", scatter_dimension=1, tiled=True)
    return result.astype(jnp.bfloat16)


def solution(mesh):
    return jax.shard_map(
        local,
        mesh=mesh,
        in_specs=(P("row", ("col", "layer")), P("row", "col"), P(), P()),
        out_specs=P("row", ("col", "layer")),
        check_vma=False,
    )
```

profile of v0, /device:TPU:20, one launch (start us, length us, event | category | flops | bytes accessed | tf_op | source)
XLA Modules:
  0.0 365.5 jit_solution(18108361089963021768)
XLA Ops:
  6.5 0.0 copy-start
  6.5 0.0 copy-start.1
  6.5 0.0 all-gather.9.cloned.1.call-start
  6.6 1.1 fusion.4
  7.7 2.3 compare_select_fusion
  10.0 0.7 constant_dynamic-slice_fusion
  10.7 0.0 all-gather.9.cloned.1.call-update
  10.7 0.0 all-gather.7.cloned.1.call-start
  10.8 0.0 copy-done
  10.8 0.2 fusion.7
  11.1 0.0 copy-done.1
  11.1 1.2 fusion
  12.2 0.0 all-gather.7.cloned.1.call-update
  12.3 0.0 all-gather.5.cloned.1.call-start
  12.3 0.7 constant_dynamic-slice_fusion.1
  13.1 0.0 all-gather.5.cloned.1.call-update
  13.1 0.0 all-gather.11.cloned.1.call-start
  13.1 31.7 %all-gather.9.cloned.1.call-done = bf16[2048,512]{1,0:T(8,128)(2,1)} async-done(((bf16[256,512]{1,0:T(8,128)(2,1)}), bf16[2048,512]{1,0:T(8,128)(2,1)}) %all-gather.9.cloned.1.call-update) | async-done | bytes 2097168 | tf_op jit(solution)/shard_map/all_gather | solution.py:44
  44.9 95.0 %all-gather.7.cloned.1.call-done = bf16[1024,2048]{1,0:T(8,128)(2,1)} async-done(((bf16[1024,128]{1,0:T(8,128)(2,1)}), bf16[1024,2048]{1,0:T(8,128)(2,1)}) %all-gather.7.cloned.1.call-update) | async-done | bytes 4194320 | tf_op jit(solution)/shard_map/all_gather | solution.py:38
  139.8 5.2 %fusion.19 = f32[1024,512]{1,0:T(8,128)S(1)} fusion(bf16[1024,2048]{1,0:T(8,128)(2,1)} %all-gather.7.cloned.1.call-done, bf16[2048,512]{1,0:T(8,128)(2,1)} %all-gather.9.cloned.1.call-done), kind=kOutput, calls=%fused_computation.41 | convolution fusion | flops 2147483648 | bytes 8388608 | tf_op jit(solution)/shard_map/dot_general | solution.py:22
  145.0 90.8 %all-reduce.1 = bf16[2,4,128,512]{3,2,1,0:T(8,128)(2,1)S(1)} all-reduce(f32[2,4,128,512]{3,2,1,0:T(8,128)S(1)} %bitcast.10), channel_id=1, replica_groups=mesh['row'=8,'col'=16,'layer'=4] {'layer'}, use_global_device_ids=true, to_apply=%region_0.1 | all-reduce | flops 524288 | bytes 3145728 | tf_op jit(solution)/shard_map/psum | solution.py:47
  235.8 0.7 dynamic-slice_convert_fusion
  236.6 0.0 all-gather.11.cloned.1.call-update
  236.6 0.0 reduce-scatter.2.cloned.1.call-start
  236.6 30.9 %all-gather.5.cloned.1.call-done = bf16[1024,2048]{1,0:T(8,128)(2,1)} async-done(((bf16[1024,128]{1,0:T(8,128)(2,1)}), bf16[1024,2048]{1,0:T(8,128)(2,1)}) %all-gather.5.cloned.1.call-update) | async-done | bytes 4194320 | tf_op jit(solution)/shard_map/all_gather | solution.py:46
  267.5 28.2 %all-gather.11.cloned.1.call-done = bf16[2048,512]{1,0:T(8,128)(2,1)} async-done(((bf16[256,512]{1,0:T(8,128)(2,1)}), bf16[2048,512]{1,0:T(8,128)(2,1)}) %all-gather.11.cloned.1.call-update) | async-done | bytes 2097168 | tf_op jit(solution)/shard_map/all_gather | solution.py:54
  295.6 6.5 %fusion.20 = f32[1024,512]{1,0:T(8,128)} fusion(bf16[1024,2048]{1,0:T(8,128)(2,1)} %all-gather.5.cloned.1.call-done, bf16[2048,512]{1,0:T(8,128)(2,1)} %all-gather.11.cloned.1.call-done), kind=kOutput, calls=%fused_computation.42 | convolution fusion | flops 2147483648 | bytes 8388608 | tf_op jit(solution)/shard_map/dot_general | solution.py:22
  302.2 0.0 reduce-scatter.2.cloned.1.call-update
  302.2 55.0 %reduce-scatter.2.cloned.1.call-done = f32[1024,128]{1,0:T(8,128)} async-done(((f32[1024,512]{1,0:T(8,128)}), f32[1024,128]{1,0:T(8,128)}) %reduce-scatter.2.cloned.1.call-update) | async-done | bytes 524304 | tf_op jit(solution)/shard_map/reduce_scatter | solution.py:55
  357.2 1.8 convert_element_type.23
  (3 shorter events, 0.0 us)
Async XLA Ops:
  6.5 4.3 %copy-start = (s32[32,32]{1,0:T(8,128)S(1)}, s32[32,32]{1,0:T(8,128)}, u32[]{:S(2)}) copy-start(s32[32,32]{1,0:T(8,128)} %param.6) | copy-start | bytes 12292
  6.5 4.5 %copy-start.1 = (bf16[1024,128]{1,0:T(8,128)(2,1)S(1)}, bf16[1024,128]{1,0:T(8,128)(2,1)}, u32[]{:S(2)}) copy-start(bf16[1024,128]{1,0:T(8,128)(2,1)} %param.4) | copy-start | bytes 786436
  6.5 38.3 %all-gather.9.cloned.1.call-start = ((), (), s32[]{:S(2)}) async-start(), calls=%async_computation.3 | async-start | bytes 2359296 | tf_op jit(solution)/shard_map/all_gather | solution.py:44
  10.7 129.1 %all-gather.7.cloned.1.call-start = ((), (), s32[]{:S(2)}) async-start(), calls=%async_computation.2 | async-start | bytes 4456448 | tf_op jit(solution)/shard_map/all_gather | solution.py:38
  12.3 255.2 %all-gather.5.cloned.1.call-start = ((), (), s32[]{:S(2)}) async-start(), calls=%async_computation.1 | async-start | bytes 4456448 | tf_op jit(solution)/shard_map/all_gather | solution.py:46
  13.1 282.6 %all-gather.11.cloned.1.call-start = ((), (), s32[]{:S(2)}) async-start(), calls=%async_computation.4 | async-start | bytes 2359296 | tf_op jit(solution)/shard_map/all_gather | solution.py:54
  236.6 120.7 %reduce-scatter.2.cloned.1.call-start = ((), (), s32[]{:S(2)}) async-start(), calls=%async_computation.5 | async-start | bytes 2621440 | tf_op jit(solution)/shard_map/reduce_scatter | solution.py:55
Sparse Core Ops, SparseCore 0:
  10.9 33.9 all-gather.8
  46.9 92.9 all-gather.6
  141.9 125.5 all-gather.4
  269.5 26.1 all-gather.10
  302.3 54.8 reduce-scatter.1
where the time goes:
time: 366 us
  waiting for transfers between devices  241 us (66%)
  blocking collectives  90.8 us (25%)
  matrix products  16.5 us (5%)
  between operations  13.2 us (4%)
    all_gather x1, waiting for transfers between devices, local(): h_whole = lax.all_gather(h_local, 'col', axis=1, tiled=True)  95 us
    psum x1, blocking collectives, local(): summed = lax.psum(partial_y, 'layer')  90.8 us
    reduce_scatter x1, waiting for transfers between devices, local(): lax.psum_scatter(partial_c, 'layer', scatter_dimension=1, tiled=True)  55 us
    all_gather x1, waiting for transfers between devices, local(): lax.all_gather(z_part, 'row', axis=0, tiled=True)  31.7 us
    all_gather x1, waiting for transfers between devices, local(): z_rows = lax.all_gather(z_quarter, 'col', axis=1, tiled=True)  30.9 us
    all_gather x1, waiting for transfers between devices, local(): lax.all_gather(y_own, 'row', axis=0, tiled=True)  28.2 us
    dot_general x2, matrix products, accumulate(): return jnp.dot(left, right, preferred_element_type=jnp.float32)  11.7 us
  transfers between devices with their start and end apart: 5, of which 5 were waited for; matrix products, arithmetic and copies ran while one was open for 2% of the time, Pallas kernels for 0%

commit v1 on v0

--- a/solution.py
+++ b/solution.py
@@ -4,6 +4,15 @@
 from jax.sharding import PartitionSpec as P
 
 BS = 256
+derive_the_words = lambda inp, axis_k: jnp.concatenate(
+    lax.all_to_all(
+        jnp.stack([inp for _ in range(lax.axis_size("row"))], 0),
+        axis_name="row",
+        split_axis=0,
+        concat_axis=0,
+    ),
+    axis_k,
+)
 
 
 def mask_tile(tile, pattern, row_start, col_start):
@@ -41,7 +50,7 @@
         per_row * quarter, cols_here
     )
     columns = h_whole
-    partial_y = accumulate(columns, lax.all_gather(z_part, "row", axis=0, tiled=True))
+    partial_y = accumulate(columns, derive_the_words(z_part, 0))
     z_quarter = lax.dynamic_slice_in_dim(z_local, layer_index * quarter, quarter, 1)
     z_rows = lax.all_gather(z_quarter, "col", axis=1, tiled=True)
     summed = lax.psum(partial_y, "layer")

time: 366 us -> 332 us (0.907)
  waiting for transfers between devices: 241 us -> 176 us
  blocking collectives: 90.8 us -> 120 us
    all_gather x1, waiting for transfers between devices: 95 us -> 62.3 us  [local(): h_whole = lax.all_gather(h_local, 'col', axis=1, tiled=True)]
    all_gather x1 -> x0, waiting for transfers between devices: 31.7 us -> none  [local(): lax.all_gather(z_part, 'row', axis=0, tiled=True)]
    all_to_all x0 -> x1, blocking collectives: none -> 29 us  [lax.all_to_all(jnp.stack([inp for _ in range(lax.axis_size('row'))], 0),...]
  transfers between devices with their start and end apart: 5 -> 4, of which waited for: 5 -> 4; matrix products, arithmetic and copies ran while one was open for 2% -> 3% of each run, Pallas kernels for 0% -> 0%
where the time goes in v1:
time: 332 us; the launch traced here: 331 us
  waiting for transfers between devices  176 us (53%)
  blocking collectives  120 us (36%)
  matrix products  18.1 us (5%)
  between operations  13.2 us (4%)
    psum x1, blocking collectives, local(): summed = lax.psum(partial_y, 'layer')  91.1 us
    all_gather x1, waiting for transfers between devices, local(): h_whole = lax.all_gather(h_local, 'col', axis=1, tiled=True)  62.3 us
    reduce_scatter x1, waiting for transfers between devices, local(): lax.psum_scatter(partial_c, 'layer', scatter_dimension=1, tiled=True)  55 us
    all_gather x1, waiting for transfers between devices, local(): z_rows = lax.all_gather(z_quarter, 'col', axis=1, tiled=True)  32.6 us
    all_to_all x1, blocking collectives, lax.all_to_all(jnp.stack([inp for _ in range(lax.axis_size('row'))], 0),...  29 us
    all_gather x1, waiting for transfers between devices, local(): lax.all_gather(y_own, 'row', axis=0, tiled=True)  26.2 us
    dot_general x2, matrix products, accumulate(): return jnp.dot(left, right, preferred_element_type=jnp.float32)  11.7 us
  transfers between devices with their start and end apart: 4, of which 4 were waited for; matrix products, arithmetic and copies ran while one was open for 3% of the time, Pallas kernels for 0%

profile of v1, /device:TPU:20, one launch (start us, length us, event | category | flops | bytes accessed | tf_op | source)
XLA Modules:
  0.0 331.3 jit_solution(8961672739624774602)
XLA Ops:
  6.5 0.0 all-gather.6.cloned.1.call-start
  6.6 1.0 fusion.7
  7.5 2.1 fusion
  9.7 0.0 all-gather.6.cloned.1.call-update
  9.7 0.0 all-gather.4.cloned.1.call-start
  9.7 1.0 fusion.4
  10.8 2.3 compare_select_fusion
  13.1 0.7 constant_dynamic-slice_fusion.1
  13.9 0.0 all-gather.4.cloned.1.call-update
  13.9 0.0 all-gather.8.cloned.1.call-start
  14.0 0.2 stack.3
  14.1 29.0 %all_to_all.5 = bf16[8,256,512]{2,1,0:T(8,128)(2,1)} all-to-all(bf16[8,256,512]{2,1,0:T(8,128)(2,1)S(1)} %stack.3), channel_id=1, replica_groups=mesh['row'=8,'col'=16,'layer'=4] {'row'}, dimensions={0} | all-to-all | bytes 4194304 | tf_op jit(solution)/shard_map/all_to_all | solution.py:8
  43.2 62.3 %all-gather.6.cloned.1.call-done = bf16[1024,2048]{1,0:T(8,128)(2,1)} async-done(((bf16[1024,128]{1,0:T(8,128)(2,1)}), bf16[1024,2048]{1,0:T(8,128)(2,1)}) %all-gather.6.cloned.1.call-update) | async-done | bytes 4194320 | tf_op jit(solution)/shard_map/all_gather | solution.py:47
  105.5 5.2 %fusion.19 = f32[1024,512]{1,0:T(8,128)S(1)} fusion(bf16[1024,2048]{1,0:T(8,128)(2,1)} %all-gather.6.cloned.1.call-done, bf16[2048,512]{1,0:T(8,128)(2,1)} %bitcast.12), kind=kOutput, calls=%fused_computation.41 | convolution fusion | flops 2147483648 | bytes 8388608 | tf_op jit(solution)/shard_map/dot_general | solution.py:31
  110.7 91.1 %all-reduce.1 = bf16[2,4,128,512]{3,2,1,0:T(8,128)(2,1)S(1)} all-reduce(f32[2,4,128,512]{3,2,1,0:T(8,128)S(1)} %bitcast.11), channel_id=1, replica_groups=mesh['row'=8,'col'=16,'layer'=4] {'layer'}, use_global_device_ids=true, to_apply=%region_0.1 | all-reduce | flops 524288 | bytes 3145728 | tf_op jit(solution)/shard_map/psum | solution.py:56
  201.8 0.7 dynamic-slice_convert_fusion
  202.5 0.0 all-gather.8.cloned.1.call-update
  202.6 0.0 reduce-scatter.2.cloned.1.call-start
  202.6 32.6 %all-gather.4.cloned.1.call-done = bf16[1024,2048]{1,0:T(8,128)(2,1)} async-done(((bf16[1024,128]{1,0:T(8,128)(2,1)}), bf16[1024,2048]{1,0:T(8,128)(2,1)}) %all-gather.4.cloned.1.call-update) | async-done | bytes 4194320 | tf_op jit(solution)/shard_map/all_gather | solution.py:55
  235.2 26.2 %all-gather.8.cloned.1.call-done = bf16[2048,512]{1,0:T(8,128)(2,1)} async-done(((bf16[256,512]{1,0:T(8,128)(2,1)}), bf16[2048,512]{1,0:T(8,128)(2,1)}) %all-gather.8.cloned.1.call-update) | async-done | bytes 2097168 | tf_op jit(solution)/shard_map/all_gather | solution.py:63
  261.4 6.5 %fusion.20 = f32[1024,512]{1,0:T(8,128)} fusion(bf16[1024,2048]{1,0:T(8,128)(2,1)} %all-gather.4.cloned.1.call-done, bf16[2048,512]{1,0:T(8,128)(2,1)} %all-gather.8.cloned.1.call-done), kind=kOutput, calls=%fused_computation.42 | convolution fusion | flops 2147483648 | bytes 8388608 | tf_op jit(solution)/shard_map/dot_general | solution.py:31
  267.9 0.0 reduce-scatter.2.cloned.1.call-update
  268.0 55.0 %reduce-scatter.2.cloned.1.call-done = f32[1024,128]{1,0:T(8,128)} async-done(((f32[1024,512]{1,0:T(8,128)}), f32[1024,128]{1,0:T(8,128)}) %reduce-scatter.2.cloned.1.call-update) | async-done | bytes 524304 | tf_op jit(solution)/shard_map/reduce_scatter | solution.py:64
  323.0 1.8 convert_element_type.23
  (4 shorter events, 0.1 us)
Async XLA Ops:
  6.5 98.9 %all-gather.6.cloned.1.call-start = ((), (), s32[]{:S(2)}) async-start(), calls=%async_computation.3 | async-start | bytes 4456448 | tf_op jit(solution)/shard_map/all_gather | solution.py:47
  9.7 225.5 %all-gather.4.cloned.1.call-start = ((), (), s32[]{:S(2)}) async-start(), calls=%async_computation.2 | async-start | bytes 4456448 | tf_op jit(solution)/shard_map/all_gather | solution.py:55
  13.9 247.5 %all-gather.8.cloned.1.call-start = ((), (), s32[]{:S(2)}) async-start(), calls=%async_computation.4 | async-start | bytes 2359296 | tf_op jit(solution)/shard_map/all_gather | solution.py:63
  202.6 120.5 %reduce-scatter.2.cloned.1.call-start = ((), (), s32[]{:S(2)}) async-start(), calls=%async_computation.5 | async-start | bytes 2621440 | tf_op jit(solution)/shard_map/reduce_scatter | solution.py:64
Sparse Core Ops, SparseCore 0:
  9.8 95.6 all-gather.5
  107.5 127.6 all-gather.3
  237.3 24.0 all-gather.7
  268.1 54.8 reduce-scatter.1

commit v2 on v0

--- a/solution.py
+++ b/solution.py
@@ -44,7 +44,7 @@
     partial_y = accumulate(columns, lax.all_gather(z_part, "row", axis=0, tiled=True))
     z_quarter = lax.dynamic_slice_in_dim(z_local, layer_index * quarter, quarter, 1)
     z_rows = lax.all_gather(z_quarter, "col", axis=1, tiled=True)
-    summed = lax.psum(partial_y, "layer")
+    summed = jax.lax.all_gather(partial_y, axis_name="layer").sum(axis=0)
     layered = summed.reshape(per_row, layers, quarter, cols_here)
     own_rows = lax.dynamic_index_in_dim(layered, layer_index, 1, keepdims=False).reshape(
         per_row * quarter, cols_here

time: 366 us -> 497 us (1.36)
  the two profiles are of different devices: /device:TPU:20 before, /device:TPU:22 now
where the time goes in v2:
time: 497 us
  waiting for transfers between devices  457 us (92%)
  matrix products  17.8 us (4%)
  between operations  13.5 us (3%)
  other arithmetic  6.37 us (1%)
    all_gather x1, waiting for transfers between devices, local(): summed = jax.lax.all_gather(partial_y, axis_name='layer').sum(axis=0)  153 us
    all_gather x1, waiting for transfers between devices, local(): h_whole = lax.all_gather(h_local, 'col', axis=1, tiled=True)  95 us
    all_gather x1, waiting for transfers between devices, local(): z_rows = lax.all_gather(z_quarter, 'col', axis=1, tiled=True)  91.5 us
    reduce_scatter x1, waiting for transfers between devices, local(): lax.psum_scatter(partial_c, 'layer', scatter_dimension=1, tiled=True)  55 us
    all_gather x1, waiting for transfers between devices, local(): lax.all_gather(z_part, 'row', axis=0, tiled=True)  32.5 us
    all_gather x1, waiting for transfers between devices, local(): lax.all_gather(y_own, 'row', axis=0, tiled=True)  30.4 us
    dot_general x2, matrix products, accumulate(): return jnp.dot(left, right, preferred_element_type=jnp.float32)  13 us
  transfers between devices with their start and end apart: 6, of which 6 were waited for; matrix products, arithmetic and copies ran while one was open for 2% of the time, Pallas kernels for 0%

profile of v2, /device:TPU:22, one launch (start us, length us, event | category | flops | bytes accessed | tf_op | source)
XLA Modules:
  0.0 497.2 jit_solution(2216060005166319755)
XLA Ops:
  6.5 0.0 copy-start
  6.5 0.0 copy-start.1
  6.5 0.0 all-gather.11.cloned.1.call-start
  6.6 1.1 fusion.4
  7.7 2.3 compare_select_fusion
  10.0 0.7 constant_dynamic-slice_fusion
  10.7 0.0 all-gather.11.cloned.1.call-update
  10.7 0.0 all-gather.9.cloned.1.call-start
  10.8 0.0 copy-done
  10.8 0.2 fusion.7
  11.0 0.0 copy-done.1
  11.1 1.2 fusion
  12.2 0.0 all-gather.9.cloned.1.call-update
  12.2 0.0 all-gather.15.cloned.1.call-start
  12.3 32.5 %all-gather.11.cloned.1.call-done = bf16[2048,512]{1,0:T(8,128)(2,1)} async-done(((bf16[256,512]{1,0:T(8,128)(2,1)}), bf16[2048,512]{1,0:T(8,128)(2,1)}) %all-gather.11.cloned.1.call-update) | async-done | bytes 2097168 | tf_op jit(solution)/shard_map/all_gather | solution.py:44
  44.8 95.0 %all-gather.9.cloned.1.call-done = bf16[1024,2048]{1,0:T(8,128)(2,1)} async-done(((bf16[1024,128]{1,0:T(8,128)(2,1)}), bf16[1024,2048]{1,0:T(8,128)(2,1)}) %all-gather.9.cloned.1.call-update) | async-done | bytes 4194320 | tf_op jit(solution)/shard_map/all_gather | solution.py:38
  139.8 6.5 %fusion.19 = f32[1024,512]{1,0:T(8,128)} fusion(bf16[1024,2048]{1,0:T(8,128)(2,1)} %all-gather.9.cloned.1.call-done, bf16[2048,512]{1,0:T(8,128)(2,1)} %all-gather.11.cloned.1.call-done), kind=kOutput, calls=%fused_computation.41 | convolution fusion | flops 2147483648 | bytes 8388608 | tf_op jit(solution)/shard_map/dot_general | solution.py:22
  146.3 0.0 all-gather.15.cloned.1.call-update
  146.3 0.0 all-gather.7.cloned.1.call-start
  146.4 0.7 constant_dynamic-slice_fusion.1
  147.1 0.0 all-gather.7.cloned.1.call-update
  147.2 0.0 all-gather.13.cloned.1.call-start
  147.2 152.5 %all-gather.15.cloned.1.call-done = f32[4096,512]{1,0:T(8,128)} async-done(((f32[1024,512]{1,0:T(8,128)}), f32[4096,512]{1,0:T(8,128)}) %all-gather.15.cloned.1.call-update) | async-done | bytes 8388624 | tf_op jit(solution)/shard_map/all_gather | solution.py:47
  299.7 4.6 reduce_sum.9
  304.3 0.7 dynamic-slice_convert_fusion
  305.1 0.0 all-gather.13.cloned.1.call-update
  305.1 0.0 reduce-scatter.2.cloned.1.call-start
  305.1 91.5 %all-gather.7.cloned.1.call-done = bf16[1024,2048]{1,0:T(8,128)(2,1)} async-done(((bf16[1024,128]{1,0:T(8,128)(2,1)}), bf16[1024,2048]{1,0:T(8,128)(2,1)}) %all-gather.7.cloned.1.call-update) | async-done | bytes 4194320 | tf_op jit(solution)/shard_map/all_gather | solution.py:46
  396.6 30.4 %all-gather.13.cloned.1.call-done = bf16[2048,512]{1,0:T(8,128)(2,1)} async-done(((bf16[256,512]{1,0:T(8,128)(2,1)}), bf16[2048,512]{1,0:T(8,128)(2,1)}) %all-gather.13.cloned.1.call-update) | async-done | bytes 2097168 | tf_op jit(solution)/shard_map/all_gather | solution.py:54
  427.0 6.5 %fusion.20 = f32[1024,512]{1,0:T(8,128)} fusion(bf16[1024,2048]{1,0:T(8,128)(2,1)} %all-gather.7.cloned.1.call-done, bf16[2048,512]{1,0:T(8,128)(2,1)} %all-gather.13.cloned.1.call-done), kind=kOutput, calls=%fused_computation.42 | convolution fusion | flops 2147483648 | bytes 8388608 | tf_op jit(solution)/shard_map/dot_general | solution.py:22
  433.5 0.0 reduce-scatter.2.cloned.1.call-update
  433.6 55.0 %reduce-scatter.2.cloned.1.call-done = f32[1024,128]{1,0:T(8,128)} async-done(((f32[1024,512]{1,0:T(8,128)}), f32[1024,128]{1,0:T(8,128)}) %reduce-scatter.2.cloned.1.call-update) | async-done | bytes 524304 | tf_op jit(solution)/shard_map/reduce_scatter | solution.py:55
  488.6 1.8 convert_element_type.23
  (3 shorter events, 0.0 us)
Async XLA Ops:
  6.5 4.3 copy-start
  6.5 4.5 copy-start.1
  6.5 38.3 %all-gather.11.cloned.1.call-start = ((), (), s32[]{:S(2)}) async-start(), calls=%async_computation.3 | async-start | bytes 2359296 | tf_op jit(solution)/shard_map/all_gather | solution.py:44
  10.7 129.1 %all-gather.9.cloned.1.call-start = ((), (), s32[]{:S(2)}) async-start(), calls=%async_computation.2 | async-start | bytes 4456448 | tf_op jit(solution)/shard_map/all_gather | solution.py:38
  12.2 287.5 %all-gather.15.cloned.1.call-start = ((), (), s32[]{:S(2)}) async-start(), calls=%async_computation.6 | async-start | bytes 10485760 | tf_op jit(solution)/shard_map/all_gather | solution.py:47
  146.3 250.3 %all-gather.7.cloned.1.call-start = ((), (), s32[]{:S(2)}) async-start(), calls=%async_computation.1 | async-start | bytes 4456448 | tf_op jit(solution)/shard_map/all_gather | solution.py:46
  147.2 279.9 %all-gather.13.cloned.1.call-start = ((), (), s32[]{:S(2)}) async-start(), calls=%async_computation.4 | async-start | bytes 2359296 | tf_op jit(solution)/shard_map/all_gather | solution.py:54
  305.1 183.5 %reduce-scatter.2.cloned.1.call-start = ((), (), s32[]{:S(2)}) async-start(), calls=%async_computation.5 | async-start | bytes 2621440 | tf_op jit(solution)/shard_map/reduce_scatter | solution.py:55
Sparse Core Ops, SparseCore 0:
  10.8 33.9 all-gather.10
  46.8 92.9 all-gather.8
  146.5 153.2 all-gather.14
  301.6 94.9 all-gather.6
  398.6 28.3 all-gather.12
  433.7 54.8 reduce-scatter.1
